TPU v7x, 32 devices: a whole 2x2x4 slice. The times are simulated.
32 devices in a mesh: rep: 2 (over y), dom: 16 (over z, x, core).
Axes of the slice: x: 2, y: 2, z: 4, core: 2. Of those that a mesh axis runs over, the one named last changes fastest.
Arguments:
- feats: bfloat16 [4096, 256], P(('rep', 'dom')), may hold values from -6 to 6
- w_self: bfloat16 [256, 256], replicated, may hold values from -0.375 to 0.375
- w_neigh: bfloat16 [256, 256], replicated, may hold values from -1.5 to 1.5
- tile_vals: bfloat16 [2, 16, 8, 128, 128], P('rep', 'dom'), may hold values from 0 to 1
- tile_owner: int32 [2, 16, 8], P('rep', 'dom'), may hold values from 0 to 15, as said below
- tile_src: int32 [2, 16, 8], P('rep', 'dom'), may hold values from 0 to 1
- tile_count: int32 [2, 16], P('rep', 'dom'), may hold values from 4 to 8, as said below
- d_out: bfloat16 [4096, 256], P(('rep', 'dom')), may hold values from -6 to 6
Outputs:
- out_feats: bfloat16 [4096, 256], P(('rep', 'dom'))
- d_feats: bfloat16 [4096, 256], P(('rep', 'dom'))
- grad_self: float32 [256, 256], P('dom')
- grad_neigh: float32 [256, 256], P('dom')
Inputs may be any that keep to these rules, and one draw needn't show every extreme that they name: Within one list no two tiles name the same pair of tile_owner and tile_src. Tiles of list (i, j) at positions tile_count[i, j] and beyond are padding.
All inputs are finite; a program needn't handle non-finite values.
Results may differ from a plain program's by a relative error of at most 0.0049.
Values may be sent and summed in bfloat16 or wider, within the bound.
A program may use at most 128 MiB of HBM per device.

v0:
```python
import math

import jax
import jax.numpy as jnp
from jax import lax
from jax.sharding import PartitionSpec as P


def per_device(feats, w_self, w_neigh, tile_vals, tile_owner, tile_src, tile_count, d_out):
    n_dom = lax.axis_size("dom")
    rows_here, hidden = feats.shape
    tile_len = tile_vals.shape[-1]
    per_block = rows_here // tile_len
    tiles_here = tile_vals.shape[2]
    block_len = math.gcd(16, tiles_here)
    values = tile_vals[0, 0]
    owners = tile_owner[0, 0]
    sources = tile_src[0, 0]
    live_count = tile_count[0, 0]
    rounds = (live_count + block_len - 1) // block_len
    panel_rows = lax.all_gather(feats, "rep", axis=0, tiled=True)
    panel_tiles = panel_rows.reshape(-1, tile_len, hidden)

    def take_block(start):
        tile_block = lax.dynamic_slice_in_dim(values, start, block_len, 0)
        dest_rows = lax.dynamic_slice_in_dim(owners, start, block_len, 0)
        src_rows = lax.dynamic_slice_in_dim(sources, start, block_len, 0)
        live_mask = (start + jnp.arange(block_len, dtype=jnp.int32) < live_count).astype(
            jnp.float32
        )
        return (tile_block, dest_rows, src_rows, live_mask)

    def forward_round(turn_index, state_pair):
        neigh_sum, degree_sum = state_pair
        tile_block, dest_rows, src_rows, live_mask = take_block(turn_index * block_len)
        product = jnp.einsum(
            "tij,tjc->tic", tile_block, panel_tiles[src_rows], preferred_element_type=jnp.float32
        )
        neigh_sum = neigh_sum.at[dest_rows].add(product * live_mask[:, None, None])
        degree_sum = degree_sum.at[dest_rows].add(
            jnp.sum(tile_block.astype(jnp.float32), axis=2) * live_mask[:, None]
        )
        return (neigh_sum, degree_sum)

    start_sum = jnp.zeros((n_dom * per_block, tile_len, hidden), jnp.float32)
    start_deg = jnp.zeros((n_dom * per_block, tile_len), jnp.float32)
    partial_value, degree_part = lax.fori_loop(0, rounds, forward_round, (start_sum, start_deg))
    received_sums, received_deg = (
        lax.all_to_all(partial_value, "dom", split_axis=0, concat_axis=0, tiled=True),
        lax.all_to_all(degree_part, "dom", split_axis=0, concat_axis=0, tiled=True),
    )
    neigh_total = received_sums.sum(axis=0)
    degree = 1.0 + received_deg.sum(axis=0)
    mean_agg = (neigh_total / degree[:, None]).astype(jnp.bfloat16)
    pre_act = jnp.dot(feats, w_self, preferred_element_type=jnp.float32) + jnp.dot(
        mean_agg, w_neigh, preferred_element_type=jnp.float32
    )
    sigmoid_pre = jax.nn.sigmoid(pre_act)
    out_feats = (pre_act * sigmoid_pre).astype(jnp.bfloat16)
    d_pre = (
        d_out.astype(jnp.float32) * sigmoid_pre * (1.0 + pre_act * (1.0 - sigmoid_pre))
    ).astype(jnp.bfloat16)
    local_self = jnp.dot(feats.T, d_pre, preferred_element_type=jnp.float32)
    local_neigh = jnp.dot(mean_agg.T, d_pre, preferred_element_type=jnp.float32)
    row_share = hidden // n_dom
    total_self, total_neigh = lax.psum((local_self, local_neigh), ("rep", "dom"))
    row_first = lax.axis_index("dom") * row_share
    grad_self = lax.dynamic_slice_in_dim(total_self, row_first, row_share, 0)
    grad_neigh = lax.dynamic_slice_in_dim(total_neigh, row_first, row_share, 0)
    d_sum = (
        jnp.dot(d_pre, w_neigh.T, preferred_element_type=jnp.float32) / degree[:, None]
    ).astype(jnp.bfloat16)
    returned = lax.all_gather(d_sum.reshape(per_block, tile_len, hidden), "dom", axis=0, tiled=True)

    def backward_round(turn_index, grad_tiles):
        tile_block, dest_rows, src_rows, live_mask = take_block(turn_index * block_len)
        contrib = jnp.einsum(
            "tij,tic->tjc", tile_block, returned[dest_rows], preferred_element_type=jnp.float32
        )
        return grad_tiles.at[src_rows].add(contrib * live_mask[:, None, None])

    panel_grad = lax.fori_loop(0, rounds, backward_round, jnp.zeros(panel_tiles.shape, jnp.float32))
    back_sum = lax.psum_scatter(
        panel_grad.astype(jnp.bfloat16), "rep", scatter_dimension=0, tiled=True
    ).astype(jnp.float32)
    d_feats = (
        jnp.dot(d_pre, w_self.T, preferred_element_type=jnp.float32)
        + back_sum.reshape(rows_here, hidden)
    ).astype(jnp.bfloat16)
    return (out_feats, d_feats, grad_self, grad_neigh)


def solution(mesh):
    in_specs = (
        P(("rep", "dom"), None),
        P(),
        P(),
        P("rep", "dom", None, None, None),
        P("rep", "dom", None),
        P("rep", "dom", None),
        P("rep", "dom"),
        P(("rep", "dom"), None),
    )
    out_specs = (P(("rep", "dom"), None), P(("rep", "dom"), None), P("dom", None), P("dom", None))
    return jax.shard_map(
        per_device, mesh=mesh, in_specs=in_specs, out_specs=out_specs, check_vma=False
    )
```

profile of v0, /device:TPU:0, one launch (start us, length us, event | category | flops | bytes accessed | tf_op | source)
XLA Modules:
  0.0 236.5 jit_solution(15408165112840965028)
XLA Ops:
  8.0 0.0 copy-start
  8.0 0.0 copy-start.1
  8.0 0.0 copy-start.5
  8.0 0.0 copy-start.4
  8.8 6.1 %all_gather.6 = bf16[256,256]{1,0:T(8,128)(2,1)S(1)} all-gather(bf16[128,256]{1,0:T(8,128)(2,1)} %param.12), channel_id=1, replica_groups=mesh['rep'=2,'dom'=16] {'rep'}, dimensions={0}, use_global_device_ids=true | all-gather | bytes 196608 | tf_op jit(solution)/shard_map/all_gather | solution.py:21
  14.9 1.1 convert_reduce_fusion
  16.0 1.6 broadcast_in_dim.6
  17.6 0.0 copy-done.1
  17.6 0.0 copy-done.5
  17.6 0.0 copy-done.4
  17.6 6.0 %while.25 = (s32[]{:T(128)}, f32[16,128,256]{2,1,0:T(8,128)}, f32[16,128]{1,0:T(8,128)S(1)}, s32[]{:T(128)}, s32[8]{0:T(128)S(1)}, /*index=5*/s32[8]{0:T(128)S(1...) while((s32[]{:T(128)}, f32[16,128,256]{2,1,0:T(8,128)}, ...), condition=%wide.region_4.5_spmd, body=%wide.region_1.4_spmd.sunk | while | flops 67636296 | bytes 8143785 | solution.py:47
  17.6 0.6 gather_fusion
  18.2 0.7 compare_convert_fusion.4
  18.9 0.4 fusion.37
  19.2 0.3 copy.30
  19.6 3.3 %scatter_fusion = f32[16,128,256]{2,1,0:T(8,128)} fusion(f32[16,128,256]{2,1,0:T(8,128)} %get-tuple-element.375, s32[8]{0:T(128)S(1)} %get-tuple-element.354, f32[8,128,256]{2,1,0:T(8,128)S(1)} %copy.30), kind=kCustom, calls=%fused_computation.2.clone.1 | custom fusion | flops 262144 | bytes 3145760 | tf_op jit(solution)/shard_map/while/body/scatter-add | solution.py:39
  22.9 0.7 scatter_custom_fusion.10
  23.6 12.6 %all_to_all.14 = f32[16,1,128]{2,1,0:T(1,128)S(1)} all-to-all(f32[16,1,128]{2,1,0:T(1,128)S(1)} %bitcast.69), channel_id=1, replica_groups=mesh['rep'=2,'dom'=16] {'dom'}, dimensions={0} | all-to-all | bytes 16384 | tf_op jit(solution)/shard_map/all_to_all | solution.py:50
  36.2 3.8 %all-to-all-start = ((f32[16,128,256]{2,1,0:T(8,128)}), f32[16,128,256]{2,1,0:T(8,128)S(1)}, u32[]{:S(2)}, u32[]{:S(2)}) async-start(f32[16,128,256]{2,1,0:T(8,128)} %get-tuple-element.187), calls=%async_computation | async-start | bytes 4194304 | tf_op jit(solution)/shard_map/all_to_all | solution.py:49
  40.0 0.0 copy-start.6
  40.0 0.0 all-gather.3.cloned.1.call-start
  40.1 0.0 copy-done.2
  40.1 0.0 copy-done.3
  40.1 0.2 fusion.13
  40.3 40.7 %all-to-all-done = f32[16,128,256]{2,1,0:T(8,128)S(1)} async-done(((f32[16,128,256]{2,1,0:T(8,128)}), f32[16,128,256]{2,1,0:T(8,128)S(1)}, u32[]{:S(2)}, u32[]{:S(2)}) %all-to-all-start) | async-done | bytes 2097184 | tf_op jit(solution)/shard_map/all_to_all | solution.py:49
  81.1 0.1 reduce_sum.30
  81.2 0.9 multiply_convert_fusion
  82.1 0.8 fusion.8
  83.0 0.0 all-gather.3.cloned.1.call-update
  83.0 0.0 all-reduce.3.cloned.1.call-start
  83.1 0.9 convolution_bitcast_fusion
  84.0 1.0 fusion.12
  85.0 0.0 all-reduce.3.cloned.1.call-update
  85.0 0.0 reduce-scatter.2.cloned.1.call-start
  85.0 42.6 %all-gather.3.cloned.1.call-done = bf16[2048,256]{1,0:T(8,128)(2,1)} async-done(((bf16[128,256]{1,0:T(8,128)(2,1)}), bf16[2048,256]{1,0:T(8,128)(2,1)}) %all-gather.3.cloned.1.call-update) | async-done | bytes 1048592 | tf_op jit(solution)/shard_map/all_gather | solution.py:73
  127.7 1.8 gather_fusion.1
  129.5 0.3 fusion.10
  129.8 2.2 while.26
  129.9 0.7 compare_convert_fusion.5
  130.5 0.2 multiply_bitcast_fusion.2
  130.7 1.3 scatter_fusion.1
  132.0 0.7 convert_element_type.55
  132.7 0.0 reduce-scatter.2.cloned.1.call-update
  132.7 91.6 %all-reduce.3.cloned.1.call-done = (f32[256,256]{0,1:T(8,128)}, f32[256,256]{1,0:T(8,128)}) async-done(((f32[256,256]{0,1:T(8,128)}, f32[256,256]{1,0:T(8,128)}), (f32[256,256]{0,1:T(8,128)}, f32[256,256]{1,0:T(8,128)})) %all-reduce.3.cloned.1.call-update) | async-done | bytes 524304 | tf_op jit(solution)/shard_map/psum | solution.py:66
  224.3 1.0 constant_dynamic-slice_fusion.1
  225.3 0.7 copy.25
  226.0 1.3 constant_dynamic-slice_fusion
  227.3 1.7 fusion.7
  (14 shorter events, 0.1 us)
Async XLA Ops:
  8.0 73.2 %copy-start = (bf16[256,256]{1,0:T(8,128)(2,1)S(1)}, bf16[256,256]{1,0:T(8,128)(2,1)}, u32[]{:S(2)}) copy-start(bf16[256,256]{1,0:T(8,128)(2,1)} %param.14) | copy-start | bytes 393220
  8.0 9.6 %copy-start.1 = (bf16[1,1,8,128,128]{4,3,2,1,0:T(8,128)(2,1)S(1)}, bf16[1,1,8,128,128]{4,3,2,1,0:T(8,128)(2,1)}, u32[]{:S(2)}) copy-start(bf16[1,1,8,128,128]{4,3,2,1,0:T(8,128)(2,1)} %param.15) | copy-start | bytes 786436
  8.0 9.6 %copy-start.5 = (s32[1,1,8]{2,1,0:T(1,128)S(1)}, s32[1,1,8]{2,1,0:T(1,128)}, u32[]{:S(2)}) copy-start(s32[1,1,8]{2,1,0:T(1,128)} %param.17) | copy-start | bytes 100
  8.0 9.6 %copy-start.4 = (s32[1,1,8]{2,1,0:T(1,128)S(1)}, s32[1,1,8]{2,1,0:T(1,128)}, u32[]{:S(2)}) copy-start(s32[1,1,8]{2,1,0:T(1,128)} %param.16) | copy-start | bytes 100
  36.2 3.9 %copy-start.2 = (bf16[128,256]{1,0:T(8,128)(2,1)S(1)}, bf16[128,256]{1,0:T(8,128)(2,1)}, u32[]{:S(2)}) copy-start(bf16[128,256]{1,0:T(8,128)(2,1)} %param.12) | copy-start | bytes 196612
  36.2 3.9 %copy-start.3 = (bf16[256,256]{1,0:T(8,128)(2,1)S(1)}, bf16[256,256]{1,0:T(8,128)(2,1)}, u32[]{:S(2)}) copy-start(bf16[256,256]{1,0:T(8,128)(2,1)} %param.13) | copy-start | bytes 393220
  36.2 44.9 %all-to-all-start = ((f32[16,128,256]{2,1,0:T(8,128)}), f32[16,128,256]{2,1,0:T(8,128)S(1)}, u32[]{:S(2)}, u32[]{:S(2)}) async-start(f32[16,128,256]{2,1,0:T(8,128)} %get-tuple-element.187), calls=%async_computation | async-start | bytes 4194304 | tf_op jit(solution)/shard_map/all_to_all | solution.py:49
  40.0 41.2 %copy-start.6 = (bf16[128,256]{1,0:T(8,128)(2,1)S(1)}, bf16[128,256]{1,0:T(8,128)(2,1)}, u32[]{:S(2)}) copy-start(bf16[128,256]{1,0:T(8,128)(2,1)} %param.19) | copy-start | bytes 196612
  40.0 87.6 %all-gather.3.cloned.1.call-start = ((), (), s32[]{:S(2)}) async-start(), calls=%async_computation.4 | async-start | bytes 1114112 | tf_op jit(solution)/shard_map/all_gather | solution.py:73
  83.0 141.4 %all-reduce.3.cloned.1.call-start = ((), (), s32[]{:S(2)}) async-start(), calls=%async_computation.5 | async-start | bytes 1048576 | tf_op jit(solution)/shard_map/psum | solution.py:66
  85.0 142.4 %reduce-scatter.2.cloned.1.call-start = ((), (), s32[]{:S(2)}) async-start(), calls=%async_computation.3 | async-start | bytes 196608 | tf_op jit(solution)/shard_map/reduce_scatter | solution.py:83
Sparse Core Ops, SparseCore 0:
  83.1 44.4 all-gather.2
  132.8 9.2 reduce-scatter.1
Sparse Core Ops, SparseCore 1:
  88.9 135.4 all-reduce.2
where the time goes:
time: 237 us; the launch traced here: 236 us
  waiting for transfers between devices  175 us (74%)
  blocking collectives  18.7 us (8%)
  between operations  16.4 us (7%)
  other arithmetic  8.74 us (4%)
  local copies, waits for them, and re-layouts  7.34 us (3%)
  matrix products  6.17 us (3%)
  starting transfers between devices  3.97 us (2%)
    psum x1, waiting for transfers between devices, per_device(): lax.psum((local_self, local_neigh), ('rep', 'dom'))  91.6 us
    all_gather x1, waiting for transfers between devices, per_device(): lax.all_gather(d_sum.reshape(per_block, tile_len, hidden), 'dom', axis=0,...  42.6 us
    all_to_all x1, waiting for transfers between devices, per_device(): lax.all_to_all(partial_value, 'dom', split_axis=0, concat_axis=0, tiled=T...  40.7 us
    all_to_all x1, blocking collectives, per_device(): lax.all_to_all(degree_part, 'dom', split_axis=0, concat_axis=0, tiled=True)  12.6 us
    all_gather x1, blocking collectives, per_device(): panel_rows = lax.all_gather(feats, 'rep', axis=0, tiled=True)  6.14 us
  transfers between devices with their start and end apart: 4, of which 3 were waited for; matrix products, arithmetic and copies ran while one was open for 4% of the time, Pallas kernels for 0%

commit v1 on v0

v1 whole, which is shorter than its diff:
```python
import functools

import jax
import jax.numpy as jnp
from jax import lax
from jax.experimental import pallas as pl
from jax.experimental.pallas import tpu as pltpu
from jax.sharding import PartitionSpec as P

F32 = jnp.float32
BF16 = jnp.bfloat16
MESH = pl.DeviceIdType.MESH
EXTRA = 16


def dot(x, y):
    return jnp.dot(x, y, preferred_element_type=F32)


def dot_nt(x, y):
    return lax.dot_general(x, y, (((1,), (1,)), ((), ())), preferred_element_type=F32)


def dot_tn(x, y):
    return lax.dot_general(x, y, (((0,), (0,)), ((), ())), preferred_element_type=F32)


def kernel(
    dims,
    feats_ref, w_self_ref, w_neigh_ref, tiles_ref, owner_ref, src_ref, count_ref, d_out_ref,
    out_ref, d_feats_ref, g_self_ref, g_neigh_ref,
    panel, dense, dense_sib, dense_t, x_send, x_recv, own, z_send, z_recv,
    gather, f_t, m_t, f_in, m_in, w_neigh_t, grad_acc, panel_acc, back_send, back_recv,
    gr_send, gr_recv,
    panel_s, panel_r, dense_s, dense_r, xs, xr, zs, zr, gzs, gzr, gxs, gxr, gcs, gcr,
    fs, fr, ms, mr, bs, br, grs, grr,
):
    R, A, B, T, hid, tiles, share, chunk, small = dims
    n_dom = A * B * 2
    rep = lax.axis_index("rep")
    dom = lax.axis_index("dom")
    c = lax.rem(dom, 2)
    b = lax.rem(lax.div(dom, 2), B)
    a = lax.div(dom, 2 * B)

    def dom_of(aa, bb, cc):
        return (aa * B + bb) * 2 + cc

    def plus(x, k, n):
        return lax.rem(x + k, n)

    sib = dom_of(a, b, 1 - c)

    def rcopy(src, dst, s, r, to_rep, to_dom):
        return pltpu.make_async_remote_copy(
            src_ref=src, dst_ref=dst, send_sem=s, recv_sem=r,
            device_id=(to_rep, to_dom), device_id_type=MESH,
        )

    barrier = pltpu.get_barrier_semaphore()
    for k in range(1, n_dom):
        pl.semaphore_signal(barrier, inc=1, device_id=(rep, plus(dom, k, n_dom)), device_id_type=MESH)
    for k in range(1, R):
        for cc in range(2):
            pl.semaphore_signal(
                barrier, inc=1, device_id=(plus(rep, k, R), dom_of(a, b, cc)), device_id_type=MESH
            )

    keys = None
    if small:
        keys = [
            jnp.where(t < count_ref[0], owner_ref[t] * R + src_ref[t], -1) for t in range(tiles)
        ]

    def place(pair):
        if small:
            at, live = jnp.int32(0), jnp.int32(0)
            for t in range(tiles):
                hit = keys[t] == pair
                at = jnp.where(hit, t, at)
                live = jnp.where(hit, 1, live)
            return at, live

        def look(t, state):
            hit = (owner_ref[t] * R + src_ref[t] == pair) & (t < count_ref[0])
            return jnp.where(hit, t, state[0]), jnp.where(hit, 1, state[1])

        return lax.fori_loop(0, tiles, look, (jnp.int32(0), jnp.int32(0)))

    def build(cc, bb):
        def one(aa, _):
            d = dom_of(aa, bb, cc)
            for s in range(R):
                at, live = place(d * R + s)
                mask = jnp.full((T, T), live.astype(F32), F32).astype(BF16)
                dense[cc, bb, aa, :, s * T:(s + 1) * T] = tiles_ref[at] * mask
            return 0
        if small:
            for aa in range(A):
                one(aa, 0)
        else:
            lax.fori_loop(0, A, one, 0)

    for kb in list(range(1, B)) + [0]:
        build(1 - c, plus(b, kb, B))

    f_t[...] = feats_ref[...].T
    panel[c, pl.ds(pl.multiple_of(rep * T, T), T), :] = feats_ref[...]

    pl.semaphore_wait(barrier, n_dom - 1 + 2 * (R - 1))

    copies = []
    panel_in = []
    for kr in range(R):
        for kc in range(2):
            if kr == 0 and kc == 0:
                continue
            to_c = plus(c, kc, 2)
            cp = rcopy(
                feats_ref, panel.at[c, pl.ds(pl.multiple_of(rep * T, T), T)],
                panel_s.at[kr * 2 + kc], panel_r.at[kr * 2 + kc], plus(rep, R - kr, R),
                dom_of(a, b, to_c),
            )
            cp.start()
            copies.append(cp)
            panel_in.append(cp)
    dense_in = {}
    for kb in list(range(1, B)) + [0]:
        bb = plus(b, kb, B)
        cp = rcopy(dense.at[1 - c, bb], dense_sib.at[bb], dense_s.at[kb], dense_r.at[kb], rep, sib)
        cp.start()
        copies.append(cp)
        dense_in[kb] = cp

    def scatter(src, dst, s, r):
        for k in range(1, n_dom):
            to = plus(dom, k, n_dom)
            row = pl.multiple_of(lax.div(to * share, chunk) * chunk, chunk)
            cp = rcopy(src.at[pl.ds(row, chunk)], dst.at[dom], s.at[k], r.at[k], rep, to)
            cp.start()
            copies.append(cp)
        row = pl.multiple_of(lax.div(dom * share, chunk) * chunk, chunk)
        dst[dom] = src[pl.ds(row, chunk), :]

    def scatter_wait(src, dst, s, r):
        for k in range(1, n_dom):
            frm = plus(dom, n_dom - k, n_dom)
            rcopy(src.at[pl.ds(0, chunk)], dst.at[frm], s.at[k], r.at[k], rep, frm).wait_recv()

    scatter(f_t, f_in, fs, fr)
    for kb in list(range(1, B)) + [0]:
        build(c, plus(b, kb, B))

    ones = jnp.ones((EXTRA, R * T), BF16)

    def block_sum(bb, aa):
        top = dot(dense[c, bb, aa], panel[c]) + dot(dense_sib[bb, aa], panel[1 - c])
        deg = dot_nt(ones, dense[c, bb, aa]) + dot_nt(ones, dense_sib[bb, aa])
        return top, deg

    def pack(dst, top, row):
        high = row.astype(BF16)
        dst[0:T, :] = top.astype(BF16)
        dst[T:T + EXTRA, 0:T] = high
        dst[T:T + EXTRA, T:2 * T] = (row - high.astype(F32)).astype(BF16)

    for cp in panel_in:
        cp.wait_recv()
    order = [2, 3, 1, 0] if A == 4 else list(range(1, A)) + [0]
    for kb in range(1, B):
        dense_in[kb].wait_recv()
        bb = plus(b, kb, B)
        for ka in order:
            aa = plus(a, ka, A)
            top, deg = block_sum(bb, aa)
            pack(x_send.at[kb - 1, ka], top, deg)
            i = (kb - 1) * A + ka
            cp = rcopy(x_send.at[kb - 1, ka], x_recv.at[kb - 1, ka], xs.at[i], xr.at[i], rep,
                       dom_of(a, bb, c))
            cp.start()
            copies.append(cp)
    dense_in[0].wait_recv()
    for ka in order:
        top, deg = block_sum(b, plus(a, ka, A))
        own[ka, 0:T, :] = top
        own[ka, T:T + EXTRA, 0:T] = deg

    w_neigh_t[...] = w_neigh_ref[...].T
    pre_self = dot(feats_ref[...], w_self_ref[...])
    if small:
        for aa in range(A):
            for bb in range(B):
                for cc in range(2):
                    dense_t[aa, bb, :, cc * T:(cc + 1) * T] = dense[cc, bb, aa].T

    def with_x(ka):
        top = own[ka, 0:T, :]
        deg = own[ka, T:T + EXTRA, 0:T]
        for kb in range(1, B):
            i = (kb - 1) * A + ka
            rcopy(x_send.at[kb - 1, ka], x_recv.at[kb - 1, ka], xs.at[i], xr.at[i], rep, sib).wait_recv()
            got = x_recv[kb - 1, ka].astype(F32)
            top = top + got[0:T]
            deg = deg + got[T:, 0:T] + got[T:, T:2 * T]
        return top, deg

    for ka in order[:-1]:
        top, deg = with_x(ka)
        pack(z_send.at[ka], top, deg)
        cp = rcopy(z_send.at[ka], z_recv.at[ka], zs.at[ka], zr.at[ka], rep,
                   dom_of(plus(a, ka, A), b, c))
        cp.start()
        copies.append(cp)
    top, deg = with_x(0)
    for ka in order[:-1]:
        rcopy(z_send.at[ka], z_recv.at[ka], zs.at[ka], zr.at[ka], rep, sib).wait_recv()
        got = z_recv[ka].astype(F32)
        top = top + got[0:T]
        deg = deg + got[T:, 0:T] + got[T:, T:2 * T]

    inv = 1.0 / (1.0 + deg)

    def as_column(row):
        col = jnp.broadcast_to(row[0:1, :], (T, T)).T
        return jnp.concatenate([col] * (hid // T), axis=1)

    mean = (top * as_column(inv)).astype(BF16)
    pre = pre_self + dot(mean, w_neigh_ref[...])
    g = jax.nn.sigmoid(pre)
    d_pre = (d_out_ref[...].astype(F32) * g * (1.0 + pre * (1.0 - g))).astype(BF16)
    mine = gather.at[a, b, c]
    pack(mine, d_pre, inv)

    def send_a(ka):
        cp = rcopy(mine, mine, gzs.at[ka], gzr.at[ka], rep, dom_of(plus(a, ka, A), b, c))
        cp.start()
        copies.append(cp)

    def block_at(ka, kb, cc):
        return gather.at[plus(a, A - ka, A), plus(b, B - kb, B), cc]

    def send_b(ka):
        blk = block_at(ka, 0, c)
        for kb in range(1, B):
            i = kb * A + ka
            cp = rcopy(blk, blk, gxs.at[i], gxr.at[i], rep, dom_of(a, plus(b, kb, B), c))
            cp.start()
            copies.append(cp)

    def send_c(ka, kb):
        blk = block_at(ka, kb, c)
        i = kb * A + ka
        cp = rcopy(blk, blk, gcs.at[i], gcr.at[i], rep, sib)
        cp.start()
        copies.append(cp)

    for ka in order[:-1]:
        send_a(ka)
    send_b(0)
    send_c(0, 0)
    out_ref[...] = (pre * g).astype(BF16)
    m_t[...] = mean.T
    scatter(m_t, m_in, ms, mr)
    d_self = dot_nt(d_pre, w_self_ref[...])

    panel_acc[...] = jnp.zeros_like(panel_acc)
    grad_acc[...] = jnp.zeros_like(grad_acc)

    def wait_c(ka, kb):
        blk = block_at(ka, kb, 1 - c)
        i = kb * A + ka
        rcopy(blk, blk, gcs.at[i], gcr.at[i], rep, sib).wait_recv()

    def use_pair(ka, kb):
        wait_c(ka, kb)
        aa, bb = plus(a, A - ka, A), plus(b, B - kb, B)
        d = [gather[aa, bb, cc, 0:T, :] for cc in range(2)]
        both = jnp.concatenate(d, axis=0)
        cols = []
        for cc in range(2):
            row = gather[aa, bb, cc, T:T + EXTRA, :].astype(F32)
            cols.append(as_column(row[:, 0:T] + row[:, T:2 * T]))
        d_sum = (dot(both, w_neigh_t[...]) * jnp.concatenate(cols, axis=0)).astype(BF16)
        if small:
            panel_acc[...] += dot(dense_t[aa, bb], d_sum)
        else:
            for cc in range(2):
                for s in range(R):
                    panel_acc[s * T:(s + 1) * T, :] += dot_tn(
                        dense[cc, bb, aa, :, s * T:(s + 1) * T], d_sum[cc * T:(cc + 1) * T]
                    )

    later = []
    for ka in [0] + order[:-1]:
        if ka > 0:
            blk = block_at(ka, 0, c)
            rcopy(blk, blk, gzs.at[ka], gzr.at[ka], rep, sib).wait_recv()
            send_b(ka)
            send_c(ka, 0)
        for kb in range(1, B):
            blk = block_at(ka, kb, c)
            i = kb * A + ka
            rcopy(blk, blk, gxs.at[i], gxr.at[i], rep, sib).wait_recv()
            send_c(ka, kb)
        for pair in later:
            use_pair(*pair)
        later = [(ka, kb) for kb in range(B)]
    for pair in later:
        use_pair(*pair)

    back = []
    for kr in range(1, R):
        to = plus(rep, kr, R)
        rows = pl.ds(pl.multiple_of(to * T, T), T)
        back_send[kr] = panel_acc[rows, :].astype(BF16)
        cp = rcopy(back_send.at[kr], back_recv.at[kr], bs.at[kr], br.at[kr], to, dom)
        cp.start()
        back.append(cp)

    scatter_wait(f_t, f_in, fs, fr)
    scatter_wait(m_t, m_in, ms, mr)

    def grad_pair(p, _):
        aa, bb = lax.div(p, B), lax.rem(p, B)
        lhs = []
        for ref in (f_in, m_in):
            lhs.append(jnp.concatenate([ref[2 * p], ref[2 * p + 1]], axis=1))
        rhs = jnp.concatenate([gather[aa, bb, cc, 0:T, :] for cc in range(2)], axis=0)
        grad_acc[...] += dot(jnp.concatenate(lhs, axis=0), rhs)
        return 0

    if small:
        for p in range(A * B):
            grad_pair(p, 0)
    else:
        lax.fori_loop(0, A * B, grad_pair, 0)
    gr_send[...] = grad_acc[...]
    for kr in range(1, R):
        cp = rcopy(gr_send, gr_recv.at[kr], grs.at[kr], grr.at[kr], plus(rep, kr, R), dom)
        cp.start()
        back.append(cp)

    mine_rows = pl.ds(pl.multiple_of(rep * T, T), T)
    total = d_self + panel_acc[mine_rows, :]
    for kr in range(1, R):
        back[kr - 1].wait_recv()
        total = total + back_recv[kr].astype(F32)
    d_feats_ref[...] = total.astype(BF16)
    grads = grad_acc[...]
    for kr in range(1, R):
        back[R - 1 + kr - 1].wait_recv()
        grads = grads + gr_recv[kr]
    at = lax.rem(dom * share, chunk)
    for i, ref in enumerate((g_self_ref, g_neigh_ref)):
        part = grads[i * chunk:(i + 1) * chunk]
        res = part[0:share]
        for k in range(1, chunk // share):
            res = jnp.where(at == k * share, part[k * share:(k + 1) * share], res)
        ref[...] = res

    for cp in copies + back:
        cp.wait_send()


def per_device(feats, w_self, w_neigh, tile_vals, tile_owner, tile_src, tile_count, d_out):
    R = lax.axis_size("rep")
    n_dom = lax.axis_size("dom")
    A = 4
    B = n_dom // (2 * A)
    T, hid = feats.shape
    tiles = tile_vals.shape[2]
    share = hid // n_dom
    chunk = max(share, 16)
    small = tiles <= 16
    msg = T + EXTRA
    dims = (R, A, B, T, hid, tiles, share, chunk, small)
    vmem = pl.BlockSpec(memory_space=pltpu.VMEM)
    smem = pl.BlockSpec(memory_space=pltpu.SMEM)
    dma = pltpu.SemaphoreType.DMA
    scratch = [
        pltpu.VMEM((2, R * T, hid), BF16),
        pltpu.VMEM((2, B, A, T, R * T), BF16),
        pltpu.VMEM((B, A, T, R * T), BF16),
        pltpu.VMEM((A, B, R * T, 2 * T) if small else (1, 1, 16, 128), BF16),
        pltpu.VMEM((B - 1, A, msg, hid), BF16),
        pltpu.VMEM((B - 1, A, msg, hid), BF16),
        pltpu.VMEM((A, msg, hid), F32),
        pltpu.VMEM((A, msg, hid), BF16),
        pltpu.VMEM((A, msg, hid), BF16),
        pltpu.VMEM((A, B, 2, msg, hid), BF16),
        pltpu.VMEM((hid, T), BF16),
        pltpu.VMEM((hid, T), BF16),
        pltpu.VMEM((n_dom, chunk, T), BF16),
        pltpu.VMEM((n_dom, chunk, T), BF16),
        pltpu.VMEM((hid, hid), BF16),
        pltpu.VMEM((2 * chunk, hid), F32),
        pltpu.VMEM((R * T, hid), F32),
        pltpu.VMEM((R, T, hid), BF16),
        pltpu.VMEM((R, T, hid), BF16),
        pltpu.VMEM((2 * chunk, hid), F32),
        pltpu.VMEM((R, 2 * chunk, hid), F32),
        dma((2 * R,)), dma((2 * R,)),
        dma((B,)), dma((B,)),
        dma(((B - 1) * A,)), dma(((B - 1) * A,)),
        dma((A,)), dma((A,)),
        dma((A,)), dma((A,)),
        dma((A * B,)), dma((A * B,)),
        dma((A * B,)), dma((A * B,)),
        dma((n_dom,)), dma((n_dom,)),
        dma((n_dom,)), dma((n_dom,)),
        dma((R,)), dma((R,)),
        dma((R,)), dma((R,)),
    ]
    return pl.pallas_call(
        functools.partial(kernel, dims),
        out_shape=(
            jax.ShapeDtypeStruct((T, hid), BF16),
            jax.ShapeDtypeStruct((T, hid), BF16),
            jax.ShapeDtypeStruct((share, hid), F32),
            jax.ShapeDtypeStruct((share, hid), F32),
        ),
        in_specs=[vmem, vmem, vmem, vmem, smem, smem, smem, vmem],
        out_specs=(vmem, vmem, vmem, vmem),
        scratch_shapes=scratch,
        compiler_params=pltpu.CompilerParams(
            collective_id=0, has_side_effects=True, vmem_limit_bytes=60 * 1024 * 1024
        ),
        name="sage_layer",
    )(
        feats, w_self, w_neigh, tile_vals[0, 0], tile_owner.reshape(-1), tile_src.reshape(-1),
        tile_count.reshape(-1), d_out,
    )


def solution(mesh):
    in_specs = (
        P(("rep", "dom"), None),
        P(),
        P(),
        P("rep", "dom", None, None, None),
        P("rep", "dom", None),
        P("rep", "dom", None),
        P("rep", "dom"),
        P(("rep", "dom"), None),
    )
    out_specs = (P(("rep", "dom"), None), P(("rep", "dom"), None), P("dom", None), P("dom", None))
    return jax.shard_map(
        per_device, mesh=mesh, in_specs=in_specs, out_specs=out_specs, check_vma=False
    )
```

time: 237 us -> 55 us (0.23)
  waiting for transfers between devices: 175 us -> 0 us
  Pallas kernels: 0 us -> 49.8 us
  blocking collectives: 18.7 us -> 0 us
  between operations: 16.4 us -> 1.3 us
  other arithmetic: 8.74 us -> 0 us
  matrix products: 6.17 us -> 0 us
  starting transfers between devices: 3.97 us -> 0 us
  local copies, waits for them, and re-layouts: 7.34 us -> 3.55 us
    psum x1 -> x0, waiting for transfers between devices: 91.6 us -> none  [per_device(): lax.psum((local_self, local_neigh), ('rep', 'dom'))]
    pallas_call x0 -> x1, Pallas kernels: none -> 49.8 us  [per_device(): pl.pallas_call(functools.partial(kernel, dims), out_shape=(jax.ShapeDtype...]
    all_gather x1 -> x0, waiting for transfers between devices: 42.6 us -> none  [per_device(): lax.all_gather(d_sum.reshape(per_block, tile_len, hidden), 'dom', axis=0,...]
    all_to_all x1 -> x0, waiting for transfers between devices: 40.7 us -> none  [per_device(): lax.all_to_all(partial_value, 'dom', split_axis=0, concat_axis=0, tiled=T...]
    all_to_all x1 -> x0, blocking collectives: 12.6 us -> none  [per_device(): lax.all_to_all(degree_part, 'dom', split_axis=0, concat_axis=0, tiled=True)]
    dot_general x8 -> x0, matrix products: 6.17 us -> none  [the longest x1 1.67 us: per_device(): jnp.dot(d_pre, w_self.T, preferred_element_type=jnp.float32)]
    all_gather x1 -> x0, blocking collectives: 6.14 us -> none  [per_device(): panel_rows = lax.all_gather(feats, 'rep', axis=0, tiled=True)]
    scatter-add x3 -> x0, other arithmetic: 5.32 us -> none  [the longest x1 3.34 us: forward_round(): neigh_sum = neigh_sum.at[dest_rows].add(product * live_mask[:, None, None])]
  transfers between devices with their start and end apart: 4 -> 0, of which waited for: 3 -> 0; matrix products, arithmetic and copies ran while one was open for 4% -> 0% of each run, Pallas kernels for 0% -> 0%
where the time goes in v1:
time: 55 us; the launch traced here: 54.7 us
  Pallas kernels  49.8 us (91%)
  local copies, waits for them, and re-layouts  3.55 us (6%)
  between operations  1.3 us (2%)
    pallas_call x1, Pallas kernels, per_device(): pl.pallas_call(functools.partial(kernel, dims), out_shape=(jax.ShapeDtype...  49.8 us
    unnamed x10, local copies, waits for them, and re-layouts  3.55 us

profile of v1, /device:TPU:0, one launch (start us, length us, event | category | flops | bytes accessed | tf_op | source)
XLA Modules:
  0.0 54.7 jit_solution(10963282648101463745)
XLA Ops:
  1.3 49.8 %sage_layer.1 = (bf16[128,256]{1,0:T(8,128)(2,1)}, bf16[128,256]{1,0:T(8,128)(2,1)}, f32[16,256]{1,0:T(8,128)}, f32[16,256]{1,0:T(8,128)}) custom-call(bf16[128,256]{1,0:T(8,128)(2,1)} %feats_ref.1, bf16[256,256]{1,0:T(8,128)(2,1)} %w_self_ref.1, bf16[256,256]{1,0:T(8,128)(2,1)} %w_neigh_ref.1, bf16[8,128,128]{2,1,0:T(8,128)(2,1)} %bitcast.5, s32[8]{0:T(128)} %bitcast.6, ...), custom_call_target="tpu_custom_call" | custom-call | tf_op jit(solution)/shard_map/sage_layer/pallas_call | solution.py:414
  51.1 0.0 copy-start
  51.1 1.5 %copy.17 = bf16[128,256]{1,0:T(8,128)(2,1)} copy(bf16[128,256]{1,0:T(8,128)(2,1)} %get-tuple-element.8) | data formatting | bytes 131072
  52.6 0.0 copy-done
  52.6 0.0 copy-start.2
  52.6 0.6 %copy.18 = bf16[128,256]{1,0:T(8,128)(2,1)} copy(bf16[128,256]{1,0:T(8,128)(2,1)S(1)} %copy-done) | data formatting | bytes 131072
  53.2 0.1 copy-done.2
  53.3 0.0 copy-start.1
  53.3 0.6 %copy.19 = f32[16,256]{1,0:T(8,128)} copy(f32[16,256]{1,0:T(8,128)S(1)} %copy-done.2) | data formatting | bytes 32768
  53.9 0.1 copy-done.1
  54.0 0.6 %copy.20 = f32[16,256]{1,0:T(8,128)} copy(f32[16,256]{1,0:T(8,128)S(1)} %copy-done.1) | data formatting | bytes 32768
Async XLA Ops:
  51.1 1.5 %copy-start = (bf16[128,256]{1,0:T(8,128)(2,1)S(1)}, bf16[128,256]{1,0:T(8,128)(2,1)}, u32[]{:S(2)}) copy-start(bf16[128,256]{1,0:T(8,128)(2,1)} %get-tuple-element.9) | copy-start | bytes 196612
  52.6 0.7 %copy-start.2 = (f32[16,256]{1,0:T(8,128)S(1)}, f32[16,256]{1,0:T(8,128)}, u32[]{:S(2)}) copy-start(f32[16,256]{1,0:T(8,128)} %get-tuple-element.10) | copy-start | bytes 49156
  53.3 0.7 %copy-start.1 = (f32[16,256]{1,0:T(8,128)S(1)}, f32[16,256]{1,0:T(8,128)}, u32[]{:S(2)}) copy-start(f32[16,256]{1,0:T(8,128)} %get-tuple-element.11) | copy-start | bytes 49156
